TPU v7x, 128 devices: a whole 4x4x4 slice. The times are simulated.
128 devices in a mesh: patch: 4 (over x_hi, core), epoch: 32 (over z, x_lo, y).
Axes of the slice: x: 4 (x_hi: 2, x_lo: 2; x = x_hi * 2 + x_lo), y: 4, z: 4, core: 2. Of those that a mesh axis runs over, the one named last changes fastest.
Arguments:
- images: bfloat16 [384, 512, 4096], P('epoch', None, 'patch'), may hold values from -8 to 8
- counts: int32 [4, 32], P('patch', 'epoch'), may hold values from 1 to 12, as said below
- slot_weight: float32 [4, 384], P('patch', 'epoch'), may hold values from 0.2 to 5
- kernel_index: int32 [4, 384, 3], P('patch', 'epoch'), may hold values from 0 to 7
- kernel_slope: float32 [4, 384], P('patch', 'epoch'), may hold values from -1 to 1
- tap_basis: float32 [8, 21], replicated, may hold values from 0 to 0.1
Outputs:
- template: bfloat16 [512, 4096], P(None, 'patch')
- differences: bfloat16 [384, 512, 4096], P('epoch', None, 'patch')
Inputs may be any that keep to these rules, and one draw needn't show every extreme that they name: `counts`: slots e with e mod 12 >= the holder's count are empty; in every patch some holder uses all 12 slots.
All inputs are finite; a program needn't handle non-finite values.
Results may differ from a plain program's by a relative error of at most 0.0022.
Values may be sent and summed in bfloat16 or wider, within the bound.
No kernel may reach another device: no remote copies, remote signals or barrier semaphores. Data moves between devices by JAX's collectives and lax.ppermute only.
A program may use at most 128 MiB of HBM per device.

v0:
```python
import jax
import jax.numpy as jnp
from jax import lax
from jax.sharding import PartitionSpec as P


def extended(block, sides, width):
    for axis, dim in sides:
        count = lax.axis_size(axis)
        forward = [(i, i + 1) for i in range(count - 1)]
        backward = [(target, source) for source, target in forward]
        low = lax.ppermute(
            lax.slice_in_dim(block, block.shape[dim] - width, None, axis=dim), axis, forward
        )
        high = lax.ppermute(lax.slice_in_dim(block, 0, width, axis=dim), axis, backward)
        block = jnp.concatenate([low, block, high], axis=dim)
    return block


def taps_band(tap_row, offsets):
    hits = offsets[..., None] == jnp.arange(tap_row.shape[0])[None, None, :]
    return jnp.sum(jnp.where(hits, tap_row[None, None, :], jnp.zeros((), jnp.bfloat16)), axis=-1)


def on_device(images, counts, slot_weight, kernel_index, kernel_slope, tap_basis):
    f32 = jnp.float32
    slots, rows, width = images.shape
    half = tap_basis.shape[1] // 2
    count = counts[0, 0]
    alive = jnp.arange(slots) < count
    live_weight = jnp.where(alive, slot_weight[0], 0.0)

    def accumulate(slot, carry):
        return carry + images[slot].astype(f32) * live_weight[slot]

    weighted = lax.fori_loop(0, slots, accumulate, jnp.zeros((rows, width), f32))
    total_weight = lax.psum(jnp.sum(live_weight), "epoch")
    padded = None
    template_full = None
    share = lax.psum_scatter(weighted, "epoch", scatter_dimension=0, tiled=True)
    owned = (share / total_weight).astype(jnp.bfloat16)
    template_full = lax.all_gather(owned, "epoch", axis=0, tiled=True)
    padded = extended(template_full, (("patch", 1),), half)
    template = padded[:, half : half + width]
    one_hot = jax.nn.one_hot(kernel_index[0], tap_basis.shape[0], dtype=f32)
    taps = jnp.einsum("esb,bt->est", one_hot, tap_basis, precision=lax.Precision.HIGHEST).astype(
        jnp.bfloat16
    )
    slopes = kernel_slope[0]
    columns = lax.axis_index("patch") * width + jnp.arange(width)
    center = width * lax.axis_size("patch") / 2
    position = (columns.astype(f32) + 0.5 - center) / center
    widened = jnp.pad(padded, ((half, 128 - half), (0, 128 - 2 * half)))
    row_tile = 128
    row_tiles = rows // 128
    upper = widened[:rows].reshape(row_tiles, 128, width + 128)
    lower = widened[128 : rows + 128].reshape(row_tiles, 128, width + 128)
    row_windows = jnp.concatenate([upper, lower], axis=1)
    tile_rows = jnp.arange(row_tile)
    window_rows = jnp.arange(row_tile + 128)
    vertical_offsets = window_rows[None, :] - tile_rows[:, None]
    window_ids = jnp.arange(256)
    tile_ids = jnp.arange(128)
    horizontal_offsets = window_ids[:, None] - tile_ids[None, :]
    tiles = width // 128

    def match_slot(slot):
        tap_set = taps[slot]
        mixing = taps_band(tap_set[0], vertical_offsets)
        vertical = jnp.einsum("rj,njw->nrw", mixing, row_windows, preferred_element_type=f32)
        vertical = vertical.reshape(rows, width + 128).astype(jnp.bfloat16)
        first = vertical[:, :width].reshape(rows, tiles, 128)
        second = vertical[:, 128:].reshape(rows, tiles, 128)
        window = jnp.concatenate([first, second], axis=-1)
        bands = jnp.concatenate(
            [taps_band(tap_set[1], horizontal_offsets), taps_band(tap_set[2], horizontal_offsets)],
            axis=1,
        )
        both = jnp.einsum("hnk,kc->hnc", window, bands, preferred_element_type=f32)
        flat = both[..., :128].reshape(rows, width)
        slanted = both[..., 128:].reshape(rows, width)
        matched = flat + slopes[slot] * position[None, :] * slanted
        return (images[slot].astype(f32) - matched).astype(jnp.bfloat16)

    results = lax.map(match_slot, jnp.arange(slots))
    differences = jnp.where(alive[:, None, None], results, jnp.zeros((), jnp.bfloat16))
    return (template, differences)


def solution(mesh):
    in_specs = (
        P("epoch", None, "patch"),
        P("patch", "epoch"),
        P("patch", "epoch"),
        P("patch", "epoch", None),
        P("patch", "epoch"),
        P(),
    )
    out_specs = (P(None, "patch"), P("epoch", None, "patch"))
    return jax.shard_map(
        on_device, mesh=mesh, in_specs=in_specs, out_specs=out_specs, check_vma=False
    )
```

profile of v0, /device:TPU:9, one launch (start us, length us, event | category | flops | bytes accessed | tf_op | source)
XLA Modules:
  0.0 632.1 jit_solution(12282625454746402116)
XLA Ops:
  9.2 40.7 %while.32 = (s32[]{:T(128)}, f32[512,1024]{1,0:T(8,128)S(1)}, bf16[12,512,1024]{2,1,0:T(8,128)(2,1)}, f32[12]{0:T(128)S(1)}) while((s32[]{:T(128)}, f32[512,1024]{1,0:T(8,128)S(1)}, bf16[12,512,1024]{2,1,0:T(8,128)(2,1)}, f32[12]{0:T(128)S(1)}) %tuple.95), condition=%wide.region_1.2_spmd.clone.clone, body=%wide.region_0.1_spmd.clone.sunk.clone | while | flops 2097155 | bytes 5242963 | solution.py:36
  9.8 2.8 bitcast_add_fusion.3
  13.1 2.8 bitcast_add_fusion.3
  16.5 2.8 bitcast_add_fusion.3
  19.9 2.8 bitcast_add_fusion.3
  23.3 2.8 bitcast_add_fusion.3
  26.7 2.8 bitcast_add_fusion.3
  30.1 2.8 bitcast_add_fusion.3
  33.5 2.8 bitcast_add_fusion.3
  36.9 2.8 bitcast_add_fusion.3
  40.3 2.8 bitcast_add_fusion.3
  43.7 2.8 bitcast_add_fusion.3
  47.1 2.8 bitcast_add_fusion.3
  51.3 66.4 %psum.7 = f32[]{:T(128)} all-reduce(f32[]{:T(128)} %get-tuple-element.348), channel_id=1, replica_groups=mesh['patch'=4,'epoch'=32] {'epoch'}, use_global_device_ids=true, to_apply=%region_4.5 | all-reduce | flops 1 | bytes 8 | tf_op jit(solution)/shard_map/psum | solution.py:37
  117.7 71.0 %reduce-scatter.2.cloned.1.call-done = f32[16,1024]{1,0:T(8,128)} async-done(((f32[512,1024]{1,0:T(8,128)}), f32[16,1024]{1,0:T(8,128)}) %reduce-scatter.2.cloned.1.call-update) | async-done | bytes 65552 | tf_op jit(solution)/shard_map/reduce_scatter | solution.py:40
  191.1 153.6 %all-gather.2.cloned.1.call-done = bf16[512,1024]{1,0:T(8,128)(2,1)} async-done(((bf16[16,1024]{1,0:T(8,128)(2,1)}), bf16[512,1024]{1,0:T(8,128)(2,1)}) %all-gather.2.cloned.1.call-update) | async-done | bytes 1048592 | tf_op jit(solution)/shard_map/all_gather | solution.py:42
  345.7 26.5 %collective-permute-start = (bf16[512,10]{1,0:T(8,128)(2,1)S(1)}, bf16[512,10]{1,0:T(8,128)(2,1)S(1)}, u32[]{:S(2)}, u32[]{:S(2)}) collective-permute-start(bf16[512,10]{1,0:T(8,128)(2,1)S(1)} %get-tuple-element.360), channel_id=1, source_target_pairs={{0,32},{32,64},{64,96},{1,33},{33,65},{65,97},{2,34},{34,66},{66,9... | collective-permute-start | bytes 30728 | tf_op jit(solution)/shard_map/ppermute | solution.py:12
  374.2 5.8 collective-permute-done.1
  380.0 3.0 concatenate.20
  385.0 228.6 %while.31 = (s32[]{:T(128)}, bf16[12,512,1024]{2,1,0:T(8,128)(2,1)}, s32[12]{0:T(128)S(1)}, bf16[12,512,1024]{2,1,0:T(8,128)(2,1)}, bf16[12,3,21]{2,1,0:T(4,128)...) while((s32[]{:T(128)}, ...), condition=%wide.region_9.10_spmd.clone.clone.clone, body=%wide.region_5.9_spmd.clone.clone.sunk.clone | while | flops 852004864 | bytes 46671136 | solution.py:85
  400.2 2.3 fusion.56
  419.2 2.3 fusion.56
  438.3 2.3 fusion.56
  613.6 10.7 %broadcast_select_fusion = bf16[12,512,1024]{2,1,0:T(8,128)(2,1)} fusion(bf16[12,512,1024]{2,1,0:T(8,128)(2,1)} %get-tuple-element.237, pred[12]{0:T(512)(128)(4,1)S(1)} %iota_compare_fusion.4), kind=kLoop, calls=%fused_computation.35 | loop fusion | flops 6291456 | bytes 25165836 | tf_op jit(solution)/shard_map/jit(_where)/select_n | solution.py:86
  (328 shorter events, 206.9 us)
Async XLA Ops:
  7.2 183.7 %copy-start = (f32[8,21]{1,0:T(8,128)S(1)}, f32[8,21]{1,0:T(8,128)}, u32[]{:S(2)}) copy-start(f32[8,21]{1,0:T(8,128)} %param.15) | copy-start | bytes 2020
  7.2 181.5 %reduce-scatter.2.cloned.1.call-start = ((), (), s32[]{:S(2)}) async-start(), calls=%async_computation.1 | async-start | bytes 2162688 | tf_op jit(solution)/shard_map/reduce_scatter | solution.py:40
  49.9 1.3 copy-start.2
  49.9 140.9 %copy-start.4 = (s32[1,12,3]{1,0,2:T(1,128)S(1)}, s32[1,12,3]{1,0,2:T(1,128)}, u32[]{:S(2)}) copy-start(s32[1,12,3]{1,0,2:T(1,128)} %param.13) | copy-start | bytes 436
  51.2 293.4 %all-gather.2.cloned.1.call-start = ((), (), s32[]{:S(2)}) async-start(), calls=%async_computation.2 | async-start | bytes 1081344 | tf_op jit(solution)/shard_map/all_gather | solution.py:42
  345.7 28.5 %collective-permute-start = (bf16[512,10]{1,0:T(8,128)(2,1)S(1)}, bf16[512,10]{1,0:T(8,128)(2,1)S(1)}, u32[]{:S(2)}, u32[]{:S(2)}) collective-permute-start(bf16[512,10]{1,0:T(8,128)(2,1)S(1)} %get-tuple-element.360), channel_id=1, source_target_pairs={{0,32},{32,64},{64,96},{1,33},{33,65},{65,97},{2,34},{34,66},{66,9... | collective-permute-start | bytes 30728 | tf_op jit(solution)/shard_map/ppermute | solution.py:12
  372.2 7.8 %collective-permute-start.1 = (bf16[512,10]{1,0:T(8,128)(2,1)S(1)}, bf16[512,10]{1,0:T(8,128)(2,1)S(1)}, u32[]{:S(2)}, u32[]{:S(2)}) collective-permute-start(bf16[512,10]{1,0:T(8,128)(2,1)S(1)} %get-tuple-element.359), channel_id=1, source_target_pairs={{32,0},{64,32},{96,64},{33,1},{65,33},{97,65},{34,2},{66,34},{98,6... | collective-permute-start | bytes 30728 | tf_op jit(solution)/shard_map/ppermute | solution.py:15
  383.4 1.6 copy-start.5
  613.6 10.7 %copy-start.3 = (bf16[512,1024]{1,0:T(8,128)(2,1)S(1)}, bf16[512,1024]{1,0:T(8,128)(2,1)}, u32[]{:S(2)}) copy-start(bf16[512,1024]{1,0:T(8,128)(2,1)} %all-gather.2.cloned.1.call-done) | copy-start | bytes 3145732
  613.6 11.7 %copy-start.1 = (f32[8,21]{1,0:T(8,128)S(1)}, f32[8,21]{1,0:T(8,128)}, u32[]{:S(2)}) copy-start(f32[8,21]{1,0:T(8,128)} %param.15) | copy-start | bytes 2020
Sparse Core Ops, SparseCore 0:
  51.3 137.3 reduce-scatter.1
  191.0 153.5 all-gather.1
where the time goes:
time: 636 us; the launch traced here: 632 us
  waiting for transfers between devices  230 us (36%)
  local copies, waits for them, and re-layouts  137 us (22%)
  other arithmetic  87.1 us (14%)
  blocking collectives  66.4 us (10%)
  matrix products  35 us (6%)
  loops' own time  33 us (5%)
  starting transfers between devices  28.5 us (4%)
  between operations  14.8 us (2%)
    all_gather x1, waiting for transfers between devices, on_device(): template_full = lax.all_gather(owned, 'epoch', axis=0, tiled=True)  154 us
    reduce_scatter x1, waiting for transfers between devices, on_device(): share = lax.psum_scatter(weighted, 'epoch', scatter_dimension=0, tiled=True)  71 us
    psum x1, blocking collectives, on_device(): total_weight = lax.psum(jnp.sum(live_weight), 'epoch')  66.4 us
    add x12, other arithmetic, accumulate(): return carry + images[slot].astype(f32) * live_weight[slot]  33.5 us
    another operation x1, loops' own time, on_device(): results = lax.map(match_slot, jnp.arange(slots))  32.8 us
    dynamic_slice x24, local copies, waits for them, and re-layouts, match_slot(): return (images[slot].astype(f32) - matched).astype(jnp.bfloat16)  31.5 us
    convert_element_type x12, other arithmetic, match_slot(): return (images[slot].astype(f32) - matched).astype(jnp.bfloat16)  27.3 us
    ppermute x1, starting transfers between devices, extended(): lax.ppermute(lax.slice_in_dim(block, block.shape[dim] - width, None, axis...  26.5 us
  transfers between devices with their start and end apart: 4, of which 3 were waited for; matrix products, arithmetic and copies ran while one was open for 0% of the time, Pallas kernels for 0%

commit v1 on v0

v1 whole, which is shorter than its diff:
```python
import functools
import jax, jax.numpy as jnp
from jax import lax
from jax.experimental import pallas as pl
from jax.experimental.pallas import tpu as pltpu
from jax.sharding import PartitionSpec as P
f32=jnp.float32; bf16=jnp.bfloat16
TAPS=21; HALF=10; LANE=128; ROWOFF=16; COLOFF=16

def bands_kernel(idx_ref, basis_ref, a_ref, b_ref, *, slots):
    d_a = lax.broadcasted_iota(jnp.int32,(128,256),1)-lax.broadcasted_iota(jnp.int32,(128,256),0)-(ROWOFF-HALF)
    d_b = lax.broadcasted_iota(jnp.int32,(256,128),0)-lax.broadcasted_iota(jnp.int32,(256,128),1)-(COLOFF-HALF)
    def body(s,_):
        ia=idx_ref[s,0]; i1=idx_ref[s,1]; i2=idx_ref[s,2]
        a=jnp.zeros((128,256),f32); b1=jnp.zeros((256,128),f32); b2=jnp.zeros((256,128),f32)
        for t in range(TAPS):
            a=jnp.where(d_a==t, basis_ref[ia,t], a)
            m=d_b==t
            b1=jnp.where(m, basis_ref[i1,t], b1)
            b2=jnp.where(m, basis_ref[i2,t], b2)
        a_ref[s]=a.astype(bf16)
        b_ref[s,:,0:128]=b1.astype(bf16)
        b_ref[s,:,128:256]=b2.astype(bf16)
        return 0
    lax.fori_loop(0,slots,body,0)

def bands(idx, basis):
    slots=idx.shape[0]
    return pl.pallas_call(functools.partial(bands_kernel,slots=slots),
        out_shape=(jax.ShapeDtypeStruct((slots,128,256),bf16),jax.ShapeDtypeStruct((slots,256,256),bf16)),
        in_specs=[pl.BlockSpec(memory_space=pltpu.SMEM)]*2,
        out_specs=(pl.BlockSpec(memory_space=pltpu.VMEM),)*2,
        compiler_params=pltpu.CompilerParams(vmem_limit_bytes=40*2**20),
        name="bands")(idx,basis)


def acc_kernel(count_ref, w_ref, img_ref, out_ref, *, slots, chunk_rows):
    total = None
    weight = 0.0
    for s in range(slots):
        wt = jnp.where(s < count_ref[0, 0], w_ref[0, s], 0.0)
        weight = weight + wt
        v = img_ref[s].astype(f32) * wt
        total = v if total is None else total + v
    rows, width = total.shape
    cols = width // LANE
    stride = (chunk_rows // 8 * cols + 1) * 8
    for q in range(rows // chunk_rows):
        for r in range(chunk_rows // 8):
            for c in range(cols):
                at = q * stride + (r * cols + c) * 8
                row = q * chunk_rows + r * 8
                out_ref[at : at + 8, :] = total[row : row + 8, c * LANE : (c + 1) * LANE]
        out_ref[(q + 1) * stride - 8 : (q + 1) * stride, :] = jnp.full((8, LANE), weight, f32)


def accumulate(counts, w, images, chunk_rows, rb=32):
    slots, rows, width = images.shape
    stride = (chunk_rows * width // LANE) + 8
    per = rb // chunk_rows
    return pl.pallas_call(
        functools.partial(acc_kernel, slots=slots, chunk_rows=chunk_rows),
        grid=(rows // rb,),
        out_shape=jax.ShapeDtypeStruct((rows // chunk_rows * stride, LANE), f32),
        in_specs=[pl.BlockSpec(memory_space=pltpu.SMEM)] * 2
        + [pl.BlockSpec((slots, rb, width), lambda i: (0, i, 0))],
        out_specs=pl.BlockSpec((per * stride, LANE), lambda i: (i, 0)),
        compiler_params=pltpu.CompilerParams(vmem_limit_bytes=40 * 2**20),
        name="accumulate",
    )(counts, w, images)


def share_kernel(x_ref, out_ref, *, parts, chunk_rows, width):
    total = x_ref[0]
    for p in range(1, parts):
        total = total + x_ref[p]
    cols = width // LANE
    tiles = chunk_rows // 8 * cols
    weight = total[tiles * 8 : tiles * 8 + 8, :]
    bands_of = []
    for r in range(chunk_rows // 8):
        bands_of.append(
            jnp.concatenate(
                [total[(r * cols + c) * 8 : (r * cols + c) * 8 + 8, :] / weight for c in range(cols)], axis=1
            )
        )
    own = jnp.concatenate(bands_of, axis=0).astype(bf16)
    for p in range(parts):
        out_ref[p] = own


def share(x, parts, chunk_rows, width):
    return pl.pallas_call(
        functools.partial(share_kernel, parts=parts, chunk_rows=chunk_rows, width=width),
        out_shape=jax.ShapeDtypeStruct((parts, chunk_rows, width), bf16),
        in_specs=[pl.BlockSpec(memory_space=pltpu.VMEM)],
        out_specs=pl.BlockSpec(memory_space=pltpu.VMEM),
        compiler_params=pltpu.CompilerParams(vmem_limit_bytes=40 * 2**20),
        name="share",
    )(x)


def match_kernel(count_ref, slope_ref, pos_ref, t_ref, lo_ref, hi_ref, a_ref, b_ref, img_ref, out_ref, tp, v, *, slots, width, rows, variant):
    n=pl.program_id(0)
    tiles=width//LANE
    @pl.when(n==0)
    def _():
        z=jnp.zeros((ROWOFF,width+LANE),bf16)
        tp[0:ROWOFF,:]=z
        tp[ROWOFF+rows:ROWOFF+rows+128-ROWOFF,:]=jnp.zeros((128-ROWOFF,width+LANE),bf16)
        for r in range(0,rows,64):
            prev=lo_ref[r:r+64,:].astype(f32)
            prev=pltpu.roll(prev,COLOFF,1)
            lane=lax.broadcasted_iota(jnp.int32,(64,LANE),1)
            for c in range(tiles+1):
                cur = t_ref[r:r+64,c*LANE:(c+1)*LANE] if c<tiles else hi_ref[r:r+64,:]
                cur=pltpu.roll(cur.astype(f32),COLOFF,1)
                tp[ROWOFF+r:ROWOFF+r+64,c*LANE:(c+1)*LANE]=jnp.where(lane<COLOFF,prev,cur).astype(bf16)
                prev=cur
    win=tp[pl.ds(pl.multiple_of(n*128,128),256),:]
    A=a_ref[...].reshape(slots*128,256)
    for j in range(0,tiles+1,2):
        w=min(2,tiles+1-j)*LANE
        v[:,j*LANE:j*LANE+w]=jnp.dot(A,win[:,j*LANE:j*LANE+w],preferred_element_type=f32).astype(bf16)
    def slot(s,_):
        r0=pl.multiple_of(s*128,128)
        @pl.when(s<count_ref[0,0])
        def _():
            sl=slope_ref[0,s]
            b=b_ref[s]
            if variant==0:
                for m in range(tiles):
                    o=jnp.dot(v[pl.ds(r0,128),m*LANE:m*LANE+256],b,preferred_element_type=f32)
                    p=pos_ref[0:1,m*LANE:(m+1)*LANE]*sl
                    out_ref[s,:,m*LANE:(m+1)*LANE]=(img_ref[s,:,m*LANE:(m+1)*LANE].astype(f32)-(o[:,:LANE]+p*o[:,LANE:])).astype(bf16)
            else:
                lhs=jnp.concatenate([v[pl.ds(r0,128),m*LANE:m*LANE+256] for m in range(tiles)],axis=0)
                o=jnp.dot(lhs,b,preferred_element_type=f32)
                for m in range(tiles):
                    p=pos_ref[0:1,m*LANE:(m+1)*LANE]*sl
                    oo=o[m*128:(m+1)*128]
                    out_ref[s,:,m*LANE:(m+1)*LANE]=(img_ref[s,:,m*LANE:(m+1)*LANE].astype(f32)-(oo[:,:LANE]+p*oo[:,LANE:])).astype(bf16)
        @pl.when(s>=count_ref[0,0])
        def _():
            out_ref[s]=jnp.zeros(out_ref.shape[1:],bf16)
        return 0
    lax.fori_loop(0,slots,slot,0)

def match(counts, slopes, pos, t, lo, hi, a, b, images, variant=0):
    slots,rows,width=images.shape
    vm=pl.BlockSpec(memory_space=pltpu.VMEM)
    sm=pl.BlockSpec(memory_space=pltpu.SMEM)
    return pl.pallas_call(functools.partial(match_kernel,slots=slots,width=width,rows=rows,variant=variant),
        grid=(rows//128,),
        out_shape=jax.ShapeDtypeStruct(images.shape,bf16),
        in_specs=[sm,sm,vm,vm,vm,vm,vm,vm,pl.BlockSpec((slots,128,width),lambda i:(0,i,0))],
        out_specs=pl.BlockSpec((slots,128,width),lambda i:(0,i,0)),
        scratch_shapes=[pltpu.VMEM((rows+128,width+LANE),bf16),pltpu.VMEM((slots*128,width+LANE),bf16)],
        compiler_params=pltpu.CompilerParams(vmem_limit_bytes=56*2**20),
        cost_estimate=pl.CostEstimate(flops=10**10,bytes_accessed=28*10**6,transcendentals=0),
        name="match")(counts,slopes,pos,t,lo,hi,a,b,images)


def on_device(images, counts, slot_weight, kernel_index, kernel_slope, tap_basis):
    slots, rows, width = images.shape
    parts = lax.axis_size("epoch")
    patches = lax.axis_size("patch")
    chunk_rows = rows // parts
    partial = accumulate(counts, slot_weight, images, chunk_rows)
    pieces = lax.all_to_all(partial, "epoch", 0, 0, tiled=True)
    copies = share(pieces.reshape(parts, -1, LANE), parts, chunk_rows, width)
    template = lax.all_to_all(copies, "epoch", 0, 0, tiled=True).reshape(rows, width)
    forward = [(i, i + 1) for i in range(patches - 1)]
    backward = [(i + 1, i) for i in range(patches - 1)]
    low = lax.ppermute(template[:, width - LANE :], "patch", forward)
    high = lax.ppermute(template[:, :LANE], "patch", backward)
    a, b = bands(kernel_index[0], tap_basis)
    columns = lax.axis_index("patch") * width + jnp.arange(width)
    center = width * patches / 2
    position = ((columns.astype(f32) + 0.5 - center) / center).reshape(1, width)
    differences = match(counts, kernel_slope, position, template, low, high, a, b, images)
    return (template, differences)


def solution(mesh):
    in_specs = (
        P("epoch", None, "patch"),
        P("patch", "epoch"),
        P("patch", "epoch"),
        P("patch", "epoch", None),
        P("patch", "epoch"),
        P(),
    )
    out_specs = (P(None, "patch"), P("epoch", None, "patch"))
    return jax.shard_map(
        on_device, mesh=mesh, in_specs=in_specs, out_specs=out_specs, check_vma=False
    )
```

time: 636 us -> 116 us (0.18)
  the two profiles are of different devices: /device:TPU:9 before, /device:TPU:7 now
where the time goes in v1:
time: 116 us; the launch traced here: 115 us
  blocking collectives  56.9 us (49%)
  Pallas kernels  43.7 us (38%)
  starting transfers between devices  6.93 us (6%)
  local copies, waits for them, and re-layouts  5.76 us (5%)
  between operations  1.37 us (1%)
    all_to_all x1, blocking collectives, on_device(): pieces = lax.all_to_all(partial, 'epoch', 0, 0, tiled=True)  37.1 us
    pallas_call x1, Pallas kernels, match(): pl.pallas_call(functools.partial(match_kernel, slots=slots, width=width,...  25.8 us
    all_to_all x1, blocking collectives, on_device(): lax.all_to_all(copies, 'epoch', 0, 0, tiled=True).reshape(rows, width)  19.8 us
    pallas_call x1, Pallas kernels, accumulate(): pl.pallas_call(functools.partial(acc_kernel, slots=slots, chunk_rows=chun...  11.2 us
    pallas_call x1, Pallas kernels, bands(): pl.pallas_call(functools.partial(bands_kernel, slots=slots), out_shape=(j...  6.56 us
    ppermute x1, starting transfers between devices, on_device(): high = lax.ppermute(template[:, :LANE], 'patch', backward)  5.63 us
    unnamed x17, local copies, waits for them, and re-layouts  5.63 us
  transfers between devices with their start and end apart: 2, of which 0 were waited for; matrix products, arithmetic and copies ran while one was open for 1% of the time, Pallas kernels for 6%

profile of v1, /device:TPU:7, one launch (start us, length us, event | category | flops | bytes accessed | tf_op | source)
XLA Modules:
  0.0 115.2 jit_solution(13391119179813082583)
XLA Ops:
  1.3 0.0 copy-start.1
  1.3 0.6 copy-done.1
  1.9 11.2 %accumulate.1 = f32[4352,128]{1,0:T(8,128)S(1)} custom-call(s32[1,1]{1,0:T(1,128)S(6)} %copy.11.count_ref, f32[1,12]{1,0:T(1,128)S(1)} %copy-done.1, bf16[12,512,1024]{2,1,0:T(8,128)(2,1)} %img_ref.3), custom_call_target="tpu_custom_call" | custom-call | tf_op jit(solution)/shard_map/accumulate/pallas_call | solution.py:61
  13.1 37.1 %all_to_all.14.x_ref = f32[32,136,128]{2,1,0:T(8,128)S(1)} all-to-all(f32[32,136,128]{2,1,0:T(8,128)S(1)} %bitcast.3), channel_id=1, replica_groups=mesh['patch'=4,'epoch'=32] {'epoch'}, dimensions={0} | all-to-all | bytes 4456448 | tf_op jit(solution)/shard_map/all_to_all | solution.py:170
  50.2 0.2 share.1
  50.4 19.8 %all_to_all.15 = bf16[32,16,1024]{2,1,0:T(8,128)(2,1)S(1)} all-to-all(bf16[32,16,1024]{2,1,0:T(8,128)(2,1)S(1)} %share.1), channel_id=1, replica_groups=mesh['patch'=4,'epoch'=32] {'epoch'}, dimensions={0} | all-to-all | bytes 2097152 | tf_op jit(solution)/shard_map/all_to_all | solution.py:172
  70.2 1.3 %collective-permute-start = (bf16[512,128]{1,0:T(8,128)(2,1)S(1)}, bf16[512,128]{1,0:T(8,128)(2,1)S(1)}, u32[]{:S(2)}, u32[]{:S(2)}) collective-permute-start(bf16[512,128]{1,0:T(8,128)(2,1)S(1)} %get-tuple-element.7), channel_id=1, source_target_pairs={{0,32},{32,64},{64,96},{1,33},{33,65},{65,97},{2,34},{34,66},{66,9... | collective-permute-start | bytes 393224 | tf_op jit(solution)/shard_map/ppermute | solution.py:175
  71.5 5.6 %collective-permute-start.1 = (bf16[512,128]{1,0:T(8,128)(2,1)S(1)}, bf16[512,128]{1,0:T(8,128)(2,1)S(1)}, u32[]{:S(2)}, u32[]{:S(2)}) collective-permute-start(bf16[512,128]{1,0:T(8,128)(2,1)S(1)} %get-tuple-element.6), channel_id=1, source_target_pairs={{32,0},{64,32},{96,64},{33,1},{65,33},{97,65},{34,2},{66,34},{98,6... | collective-permute-start | bytes 393224 | tf_op jit(solution)/shard_map/ppermute | solution.py:176
  77.2 0.0 copy-done.5
  77.2 0.1 copy.9
  77.3 0.0 copy-done
  77.3 6.6 %bands.1 = (bf16[12,128,256]{2,1,0:T(8,128)(2,1)S(1)}, bf16[12,256,256]{2,1,0:T(8,128)(2,1)S(1)}) custom-call(s32[12,3]{1,0:T(8,128)S(1)} %bitcast.4, f32[8,21]{1,0:T(8,128)S(1)} %copy-done), custom_call_target="tpu_custom_call" | custom-call | tf_op jit(solution)/shard_map/bands/pallas_call | solution.py:29
  83.9 0.0 copy-start.2
  83.9 1.1 copy-done.2
  85.0 0.9 copy-done.3
  85.9 0.6 add_multiply_fusion.pos_ref
  86.5 0.0 collective-permute-done.lo_ref
  86.5 0.0 collective-permute-done.1.hi_ref
  86.5 0.0 copy-start.7
  86.5 0.0 copy-done.4
  86.5 0.6 copy-done.6
  87.2 0.1 copy-done.7
  87.2 25.8 %match.1 = bf16[12,512,1024]{2,1,0:T(8,128)(2,1)} custom-call(s32[1,1]{1,0:T(1,128)S(6)} %copy.11.count_ref, f32[1,12]{1,0:T(1,128)} %slope_ref.1, f32[1,1024]{1,0:T(1,128)} %add_multiply_fusion.pos_ref, bf16[512,1024]{1,0:T(8,128)(2,1)} %bitcast.6, bf16[512,128]{1,0:T(8,128)(2,1)} %copy-done.6, bf16[512,128]{1,0:T(8,128)(2,1)} %copy-done.7, ...), custom_call_target="tpu_custom_call" | custom-call | flops 10000000000 | bytes 28000000 | tf_op jit(solution)/shard_map/match/pallas_call | solution.py:153
  113.0 2.3 %copy.12 = bf16[512,1024]{1,0:T(8,128)(2,1)} copy(bf16[512,1024]{1,0:T(8,128)(2,1)} %bitcast.7) | data formatting | bytes 2097152
  (6 shorter events, 0.0 us)
Async XLA Ops:
  1.3 0.7 copy-start.1
  50.2 27.0 %copy-start.5 = (s32[1,12,3]{1,0,2:T(1,128)S(1)}, s32[1,12,3]{1,0,2:T(1,128)}, u32[]{:S(2)}) copy-start(s32[1,12,3]{1,0,2:T(1,128)} %param.9) | copy-start | bytes 436
  50.2 27.1 %copy-start = (f32[8,21]{1,0:T(8,128)S(1)}, f32[8,21]{1,0:T(8,128)}, u32[]{:S(2)}) copy-start(f32[8,21]{1,0:T(8,128)} %basis_ref.1) | copy-start | bytes 2020
  70.2 16.3 %copy-start.4 = (bf16[32,16,1024]{2,1,0:T(8,128)(2,1)}, bf16[32,16,1024]{2,1,0:T(8,128)(2,1)S(1)}, u32[]{:S(2)}) copy-start(bf16[32,16,1024]{2,1,0:T(8,128)(2,1)S(1)} %all_to_all.15) | copy-start | bytes 3145732
  70.2 16.3 %collective-permute-start = (bf16[512,128]{1,0:T(8,128)(2,1)S(1)}, bf16[512,128]{1,0:T(8,128)(2,1)S(1)}, u32[]{:S(2)}, u32[]{:S(2)}) collective-permute-start(bf16[512,128]{1,0:T(8,128)(2,1)S(1)} %get-tuple-element.7), channel_id=1, source_target_pairs={{0,32},{32,64},{64,96},{1,33},{33,65},{65,97},{2,34},{34,66},{66,9... | collective-permute-start | bytes 393224 | tf_op jit(solution)/shard_map/ppermute | solution.py:175
  71.5 15.0 %collective-permute-start.1 = (bf16[512,128]{1,0:T(8,128)(2,1)S(1)}, bf16[512,128]{1,0:T(8,128)(2,1)S(1)}, u32[]{:S(2)}, u32[]{:S(2)}) collective-permute-start(bf16[512,128]{1,0:T(8,128)(2,1)S(1)} %get-tuple-element.6), channel_id=1, source_target_pairs={{32,0},{64,32},{96,64},{33,1},{65,33},{97,65},{34,2},{66,34},{98,6... | collective-permute-start | bytes 393224 | tf_op jit(solution)/shard_map/ppermute | solution.py:176
  83.9 1.2 %copy-start.2 = (bf16[12,256,256]{2,1,0:T(8,128)(2,1)}, bf16[12,256,256]{2,1,0:T(8,128)(2,1)S(1)}, u32[]{:S(2)}) copy-start(bf16[12,256,256]{2,1,0:T(8,128)(2,1)S(1)} %get-tuple-element.5.b_ref) | copy-start | bytes 4718596
  85.0 0.9 copy-start.3
  86.5 0.7 copy-start.6
  86.5 0.7 copy-start.7
